TPU v7x, 32 devices: a whole 2x2x4 slice. The times are simulated.
32 devices in a mesh: groups: 2 (over y), blk: 4 (over z), ulysses: 2 (over x), cfg: 2 (over core).
Axes of the slice: x: 2, y: 2, z: 4, core: 2. Of those that a mesh axis runs over, the one named last changes fastest.
Arguments:
- queries: bfloat16 [2, 256, 3072], P('cfg', ('groups', 'blk', 'ulysses')), parts along dimension 1, may hold values from -330 to 330
- key_now: bfloat16 [2, 256, 3072], P('cfg', ('groups', 'blk', 'ulysses')), parts along dimension 1, may hold values from -6 to 6
- value_now: bfloat16 [2, 256, 3072], P('cfg', ('groups', 'blk', 'ulysses')), parts along dimension 1, may hold values from -6 to 6
- key_stale: bfloat16 [2, 256, 3072], P('cfg', 'groups', 'ulysses'), parts along dimension 1, may hold values from -6 to 6
- value_stale: bfloat16 [2, 256, 3072], P('cfg', 'groups', 'ulysses'), parts along dimension 1, may hold values from -6 to 6
- positions: int32 [256], P(('groups', 'blk', 'ulysses')), parts along dimension 0, may hold values from 0 to 127, each once
- exponents: int32 [2, 2, 8, 24], P(None, 'cfg', 'groups', 'ulysses'), parts along dimension 2, may hold values from -9 to -4
- step_index: int32 [100], P('groups'), parts along dimension 0, may hold values from 0 to 49, each once
- step_gates: bfloat16 [50, 3072], P(None, 'ulysses'), may hold values from 0.5 to 2
Outputs:
- attended: bfloat16 [2, 256, 3072], P('cfg', ('groups', 'blk', 'ulysses')), parts along dimension 1
There are 2 independent parts, one for each index of `groups`. A program takes and returns all parts, laid end to end along the dimension named above; an argument that names none is the same for every part. Nothing has to cross between parts.
Inputs may be any that keep to these rules, and one draw needn't show every extreme that they name: positions hold every number below 128 once. step_index holds every number below 50 once.
All inputs are finite; a program needn't handle non-finite values.
Results may differ from a plain program's by a relative error of at most 0.012.
The roundings to bfloat16 on the way count: a program that leaves them out, or rounds other values in their place, can miss the bound.
Values may be sent and summed in bfloat16 or wider, within the bound.
A program may use at most 64 MiB of HBM per device.

v0:
```python
import math

import jax
import jax.numpy as jnp
from jax import lax
from jax.sharding import PartitionSpec as P

HD = 128
BLOCK = 32
GRID_H = 16
GRID_W = 16


def angles(positions):
    pair_count = HD // 2
    side_pairs = HD // 6
    frame_pairs = pair_count - 2 * side_pairs
    frame_index = (positions // (GRID_H * GRID_W)).astype(jnp.float32)
    row_index = (positions // GRID_W % GRID_H).astype(jnp.float32)
    column_index = (positions % GRID_W).astype(jnp.float32)

    def frequencies(count):
        return jnp.exp(-math.log(10000.0) * jnp.arange(count, dtype=jnp.float32) / count)

    phases = jnp.concatenate(
        [
            frame_index[:, None] * frequencies(frame_pairs)[None, :],
            row_index[:, None] * frequencies(side_pairs)[None, :],
            column_index[:, None] * frequencies(side_pairs)[None, :],
        ],
        axis=1,
    )
    return (jnp.cos(phases), jnp.sin(phases))


def rotate(source, cosine, sine):
    leading = source.shape[:-1]
    head_count = source.shape[-1] // HD
    paired = source.astype(jnp.float32).reshape(leading + (head_count, HD // 2, 2))
    real_part = paired[..., 0]
    imag_part = paired[..., 1]
    cos_part = cosine[:, None, :]
    sin_part = sine[:, None, :]
    turned = jnp.stack(
        [real_part * cos_part - imag_part * sin_part, real_part * sin_part + imag_part * cos_part],
        axis=-1,
    )
    return turned.reshape(source.shape)


def shards(
    queries,
    key_now,
    value_now,
    key_stale,
    value_stale,
    positions,
    exponents,
    step_index,
    step_gates,
):
    cosine, sine = angles(positions)
    query_turned = rotate(queries[0], cosine, sine).astype(jnp.bfloat16)
    key_turned = rotate(key_now[0], cosine, sine).astype(jnp.bfloat16)
    query_local, key_local, value_local = (
        lax.all_to_all(query_turned, "ulysses", split_axis=1, concat_axis=0, tiled=True),
        lax.all_to_all(key_turned, "ulysses", split_axis=1, concat_axis=0, tiled=True),
        lax.all_to_all(value_now[0], "ulysses", split_axis=1, concat_axis=0, tiled=True),
    )
    tok_rows = query_local.shape[0]
    feature_width = query_local.shape[1]
    head_count = feature_width // HD
    all_rows = key_stale.shape[1]
    first_row = lax.axis_index("blk") * tok_rows
    powers = jnp.repeat(jnp.exp2(exponents[:, 0].astype(jnp.float32)), BLOCK, axis=1)
    inverses = jnp.repeat(jnp.exp2(-exponents[:, 0].astype(jnp.float32)), BLOCK, axis=1)
    stale_keys = key_stale[0]
    stale_values = value_stale[0]

    def encode(current, stale, inverse):
        own_stale = lax.dynamic_slice_in_dim(stale, first_row, tok_rows, 0).astype(jnp.float32)
        own_inverse = lax.dynamic_slice_in_dim(inverse, first_row, tok_rows, 0)
        difference = (
            current.astype(jnp.float32).reshape(tok_rows, head_count, HD)
            - own_stale.reshape(tok_rows, head_count, HD)
        ) * own_inverse[:, :, None]
        return (
            jnp.clip(difference, -448.0, 448.0)
            .astype(jnp.bfloat16)
            .reshape(tok_rows, feature_width)
        )

    key_sent = encode(key_local, stale_keys, inverses[0])
    value_sent = encode(value_local, stale_values, inverses[1])
    query_heads = query_local.reshape(tok_rows, head_count, HD)
    score_scale = 1.0 / math.sqrt(HD)
    stale_scores = jnp.einsum(
        "qhd,khd->hqk",
        query_heads,
        stale_keys.reshape(all_rows, head_count, HD),
        preferred_element_type=jnp.float32,
    )
    key_whole, value_whole = (
        lax.all_gather(key_sent, "blk", axis=0, tiled=True),
        lax.all_gather(value_sent, "blk", axis=0, tiled=True),
    )
    span_rows = key_whole.shape[0]
    scaling = powers[0]
    residual = key_whole.reshape(span_rows, head_count, HD)
    scaled = (residual.astype(jnp.float32) * scaling[:, :, None]).astype(jnp.bfloat16)
    fresh_scores = jnp.einsum(
        "qhd,khd->hqk", query_heads, scaled, preferred_element_type=jnp.float32
    )
    scores = (stale_scores + fresh_scores) * score_scale
    peak_score = jnp.max(scores, axis=2, keepdims=True)
    weights = jnp.exp(scores - peak_score).astype(jnp.bfloat16)
    weight_total = jnp.sum(weights.astype(jnp.float32), axis=2)
    stale_sums = jnp.einsum(
        "hqk,khd->qhd",
        weights,
        stale_values.reshape(all_rows, head_count, HD),
        preferred_element_type=jnp.float32,
    )
    span_rows = value_whole.shape[0]
    scaling = powers[1]
    residual = value_whole.reshape(span_rows, head_count, HD)
    scaled = (residual.astype(jnp.float32) * scaling[:, :, None]).astype(jnp.bfloat16)
    fresh_sums = jnp.einsum("hqk,khd->qhd", weights, scaled, preferred_element_type=jnp.float32)
    mixture = (stale_sums + fresh_sums) / weight_total.T[:, :, None]
    gate_row = lax.dynamic_index_in_dim(step_gates, step_index[0], 0, keepdims=False).astype(
        jnp.float32
    )
    gated = (mixture * gate_row.reshape(head_count, HD)[None, :, :]).astype(jnp.bfloat16)
    restored = lax.all_to_all(
        gated.reshape(tok_rows, feature_width), "ulysses", split_axis=0, concat_axis=1, tiled=True
    )
    return restored[None]


def solution(mesh):
    return jax.shard_map(
        shards,
        mesh=mesh,
        in_specs=(
            P("cfg", ("groups", "blk", "ulysses"), None),
            P("cfg", ("groups", "blk", "ulysses"), None),
            P("cfg", ("groups", "blk", "ulysses"), None),
            P("cfg", "groups", "ulysses"),
            P("cfg", "groups", "ulysses"),
            P(("groups", "blk", "ulysses")),
            P(None, "cfg", "groups", "ulysses"),
            P("groups"),
            P(None, "ulysses"),
        ),
        out_specs=P("cfg", ("groups", "blk", "ulysses"), None),
        check_vma=False,
    )
```

profile of v0, /device:TPU:0, one launch (start us, length us, event | category | flops | bytes accessed | tf_op | source)
XLA Modules:
  0.0 70.4 jit_solution(7909560390978473822)
XLA Ops:
  0.0 0.7 %fusion.18 = (f32[16]{0:T(128)S(1)}, f32[16]{0:T(128)S(1)}, f32[16]{0:T(128)S(1)}) fusion(s32[16]{0:T(128)} %param.14), kind=kLoop, calls=%fused_computation.61 | loop fusion | flops 688 | bytes 256 | tf_op jit(solution)/shard_map/convert_element_type | solution.py:18
  1.2 1.2 %copy.80 = f32[1,16,3072]{1,2,0:T(8,128)S(1)} copy(bf16[1,16,3072]{2,1,0:T(8,128)(2,1)} %param.9) | data formatting | bytes 294912 | tf_op jit(solution)/shard_map/convert_element_type | solution.py:39
  2.4 0.3 copy.87
  2.6 4.3 %subtract_convert_fusion = (bf16[16,24,64,1]{0,3,2,1:T(2,128)(2,1)S(1)}, bf16[16,24,64,1]{0,3,2,1:T(2,128)(2,1)S(1)}, bf16[16,24,64,1]{0,3,2,1:T(2,128)(2,1)S(1)}, bf16[16,24,64,1]{0,3,2,1:T(2,128)(2,1)S(1)}) fusion(f32[16,24,64,2]{0,3,2,1:T(2,128)S(1)} %bitcast.74, f32[16,64]{0,1:T(8,128)S(1)} %copy.82, f32[16,64]{0,1:T(8,128)S(1)} %copy.81, ...), kind=kLoop, calls=%fused_computation.13 | loop fusion | flops 393216 | bytes 598016 | tf_op jit(solution)/shard_map/convert.11
  7.0 4.2 %pad_maximum_fusion = (bf16[16,24,64,2]{0,3,2,1:T(2,128)(2,1)S(1)}, bf16[16,24,64,2]{0,3,2,1:T(2,128)(2,1)S(1)}) fusion(bf16[16,24,64,1]{0,3,2,1:T(2,128)(2,1)S(1)} %get-tuple-element.9, bf16[16,24,64,1]{0,3,2,1:T(2,128)(2,1)S(1)} %get-tuple-element.10, bf16[16,24,64,1]{0,3,2,1:T(2,128)(2,1)S(1)} %get-tuple-element.6, ...), kind=kLoop, calls=%fused_computation.8 | loop fusion | flops 393216 | bytes 393216 | tf_op jit(solution)/shard_map/stack | solution.py:44
  11.2 0.9 %copy.88 = bf16[16,2,1536]{2,0,1:T(8,128)(2,1)} copy(bf16[16,2,1536]{0,2,1:T(8,128)(2,1)S(1)} %bitcast.76) | data formatting | bytes 196608 | tf_op jit(solution)/shard_map/convert_element_type | solution.py:64
  12.1 4.3 %all-to-all-start.1 = ((bf16[16,2,1536]{2,0,1:T(8,128)(2,1)}), bf16[16,2,1536]{2,0,1:T(8,128)(2,1)S(1)}, u32[]{:S(2)}, u32[]{:S(2)}) async-start(bf16[16,2,1536]{2,0,1:T(8,128)(2,1)} %copy.88), calls=%async_computation.1 | async-start | bytes 196608 | tf_op jit(solution)/shard_map/all_to_all | solution.py:67
  16.5 0.9 %copy.83 = bf16[16,2,1536]{2,0,1:T(8,128)(2,1)} copy(bf16[16,2,1536]{0,2,1:T(8,128)(2,1)S(1)} %bitcast.75) | data formatting | bytes 196608 | tf_op jit(solution)/shard_map/convert_element_type | solution.py:63
  17.4 0.2 copy.84
  17.9 0.2 copy.93
  18.2 0.7 copy.95
  19.3 0.8 %convert_reduce_fusion.1 = f32[1536]{0:T(1024)S(1)} fusion(bf16[50,1536]{1,0:T(8,128)(2,1)} %param.17, s32[]{:T(128)S(6)} %select_n.34), kind=kLoop, calls=%fused_computation.33 | loop fusion | flops 1536 | bytes 9220 | tf_op jit(solution)/shard_map/convert_element_type | solution.py:130
  20.0 0.7 %all-to-all-done.1 = bf16[16,2,1536]{2,0,1:T(8,128)(2,1)S(1)} async-done(((bf16[16,2,1536]{2,0,1:T(8,128)(2,1)}), bf16[16,2,1536]{2,0,1:T(8,128)(2,1)S(1)}, u32[]{:S(2)}, u32[]{:S(2)}) %all-to-all-start.1) | async-done | bytes 98336 | tf_op jit(solution)/shard_map/all_to_all | solution.py:67
  20.8 3.3 %all-to-all-start = ((bf16[16,2,1536]{2,0,1:T(8,128)(2,1)}), bf16[16,2,1536]{2,0,1:T(8,128)(2,1)S(1)}, u32[]{:S(2)}, u32[]{:S(2)}) async-start(bf16[16,2,1536]{2,0,1:T(8,128)(2,1)} %copy.83), calls=%async_computation | async-start | bytes 196608 | tf_op jit(solution)/shard_map/all_to_all | solution.py:66
  24.3 15.2 %all_gather.6 = bf16[128,1536]{1,0:T(8,128)(2,1)S(1)} all-gather(bf16[32,1536]{1,0:T(8,128)(2,1)S(1)} %fusion.10), channel_id=1, replica_groups=mesh['groups'=2,'blk'=4,'ulysses'=2,'cfg'=2] {'blk'}, dimensions={0}, use_global_device_ids=true | all-gather | bytes 491520 | tf_op jit(solution)/shard_map/all_gather | solution.py:104
  39.7 3.3 %all-to-all-start.2 = ((bf16[16,2,1536]{2,0,1:T(8,128)(2,1)}), bf16[16,2,1536]{2,0,1:T(8,128)(2,1)S(1)}, u32[]{:S(2)}, u32[]{:S(2)}) async-start(bf16[16,2,1536]{2,0,1:T(8,128)(2,1)} %copy.95), calls=%async_computation.2 | async-start | bytes 196608 | tf_op jit(solution)/shard_map/all_to_all | solution.py:68
  43.4 0.2 fusion.3
  43.6 0.4 convolution_bitcast_fusion.1
  44.0 0.2 convert_reduce_fusion
  44.2 3.2 %all-to-all-done.2 = bf16[16,2,1536]{2,0,1:T(8,128)(2,1)S(1)} async-done(((bf16[16,2,1536]{2,0,1:T(8,128)(2,1)}), bf16[16,2,1536]{2,0,1:T(8,128)(2,1)S(1)}, u32[]{:S(2)}, u32[]{:S(2)}) %all-to-all-start.2) | async-done | bytes 98336 | tf_op jit(solution)/shard_map/all_to_all | solution.py:68
  47.6 14.7 %all_gather.7 = bf16[128,1536]{1,0:T(8,128)(2,1)S(1)} all-gather(bf16[32,1536]{1,0:T(8,128)(2,1)S(1)} %fusion.8), channel_id=1, replica_groups=mesh['groups'=2,'blk'=4,'ulysses'=2,'cfg'=2] {'blk'}, dimensions={0}, use_global_device_ids=true | all-gather | bytes 491520 | tf_op jit(solution)/shard_map/all_gather | solution.py:105
  62.4 0.4 fusion.4
  62.9 6.7 %all_to_all.52 = bf16[2,16,1536]{2,1,0:T(8,128)(2,1)S(1)} all-to-all(bf16[2,16,1536]{2,1,0:T(8,128)(2,1)S(1)} %all_to_all.45), channel_id=1, replica_groups=mesh['groups'=2,'blk'=4,'ulysses'=2,'cfg'=2] {'ulysses'}, dimensions={0} | all-to-all | bytes 196608 | tf_op jit(solution)/shard_map/all_to_all | solution.py:134
  69.7 0.7 broadcast_in_dim.43
  (44 shorter events, 2.4 us)
Async XLA Ops:
  0.0 2.4 %copy-start.2 = (bf16[1,16,3072]{2,1,0:T(8,128)(2,1)S(1)}, bf16[1,16,3072]{2,1,0:T(8,128)(2,1)}, u32[]{:S(2)}) copy-start(bf16[1,16,3072]{2,1,0:T(8,128)(2,1)} %param.10) | copy-start | bytes 294916
  7.0 9.5 %copy-start.4 = (s32[2,1,4,12]{3,2,1,0:T(4,128)S(1)}, s32[2,1,4,12]{3,2,1,0:T(4,128)}, u32[]{:S(2)}) copy-start(s32[2,1,4,12]{3,2,1,0:T(4,128)} %param.15) | copy-start | bytes 1156
  11.2 6.3 %copy-start = (bf16[1,128,1536]{2,1,0:T(8,128)(2,1)S(1)}, bf16[1,128,1536]{2,1,0:T(8,128)(2,1)}, u32[]{:S(2)}) copy-start(bf16[1,128,1536]{2,1,0:T(8,128)(2,1)} %param.12) | copy-start | bytes 1179652
  11.2 6.7 %copy-start.1 = (bf16[1,128,1536]{2,1,0:T(8,128)(2,1)S(1)}, bf16[1,128,1536]{2,1,0:T(8,128)(2,1)}, u32[]{:S(2)}) copy-start(bf16[1,128,1536]{2,1,0:T(8,128)(2,1)} %param.13) | copy-start | bytes 1179652
  12.1 6.1 %copy-start.3 = (bf16[1,16,3072]{2,1,0:T(8,128)(2,1)S(1)}, bf16[1,16,3072]{2,1,0:T(8,128)(2,1)}, u32[]{:S(2)}) copy-start(bf16[1,16,3072]{2,1,0:T(8,128)(2,1)} %param.11) | copy-start | bytes 294916
  12.1 8.7 %all-to-all-start.1 = ((bf16[16,2,1536]{2,0,1:T(8,128)(2,1)}), bf16[16,2,1536]{2,0,1:T(8,128)(2,1)S(1)}, u32[]{:S(2)}, u32[]{:S(2)}) async-start(bf16[16,2,1536]{2,0,1:T(8,128)(2,1)} %copy.88), calls=%async_computation.1 | async-start | bytes 196608 | tf_op jit(solution)/shard_map/all_to_all | solution.py:67
  16.5 2.4 %copy-start.5 = (s32[50]{0:T(128)S(1)}, s32[50]{0:T(128)}, u32[]{:S(2)}) copy-start(s32[50]{0:T(128)} %param.16) | copy-start | bytes 604
  20.8 19.0 %all-to-all-start = ((bf16[16,2,1536]{2,0,1:T(8,128)(2,1)}), bf16[16,2,1536]{2,0,1:T(8,128)(2,1)S(1)}, u32[]{:S(2)}, u32[]{:S(2)}) async-start(bf16[16,2,1536]{2,0,1:T(8,128)(2,1)} %copy.83), calls=%async_computation | async-start | bytes 196608 | tf_op jit(solution)/shard_map/all_to_all | solution.py:66
  39.7 7.6 %all-to-all-start.2 = ((bf16[16,2,1536]{2,0,1:T(8,128)(2,1)}), bf16[16,2,1536]{2,0,1:T(8,128)(2,1)S(1)}, u32[]{:S(2)}, u32[]{:S(2)}) async-start(bf16[16,2,1536]{2,0,1:T(8,128)(2,1)} %copy.95), calls=%async_computation.2 | async-start | bytes 196608 | tf_op jit(solution)/shard_map/all_to_all | solution.py:68
where the time goes:
time: 71 us; the launch traced here: 70.4 us
  blocking collectives  36.5 us (51%)
  starting transfers between devices  11 us (15%)
  other arithmetic  10.7 us (15%)
  local copies, waits for them, and re-layouts  6.7 us (9%)
  waiting for transfers between devices  3.9 us (5%)
  matrix products  1.18 us (2%)
    all_gather x1, blocking collectives, shards(): lax.all_gather(key_sent, 'blk', axis=0, tiled=True)  15.2 us
    all_gather x1, blocking collectives, shards(): lax.all_gather(value_sent, 'blk', axis=0, tiled=True)  14.7 us
    all_to_all x1, blocking collectives, shards(): lax.all_to_all(gated.reshape(tok_rows, feature_width), 'ulysses', split_a...  6.65 us
    all_to_all x1, starting transfers between devices, shards(): lax.all_to_all(key_turned, 'ulysses', split_axis=1, concat_axis=0, tiled=...  4.34 us
    another operation x1, other arithmetic  4.33 us
    another operation x1, other arithmetic, rotate(): jnp.stack([real_part * cos_part - imag_part * sin_part, real_part * sin_p...  4.18 us
    all_to_all x1, starting transfers between devices, shards(): lax.all_to_all(value_now[0], 'ulysses', split_axis=1, concat_axis=0, tile...  3.35 us
    all_to_all x1, starting transfers between devices, shards(): lax.all_to_all(query_turned, 'ulysses', split_axis=1, concat_axis=0, tile...  3.34 us
  transfers between devices with their start and end apart: 3, of which 2 were waited for; matrix products, arithmetic and copies ran while one was open for 7% of the time, Pallas kernels for 0%

commit v1 on v0

--- a/solution.py
+++ b/solution.py
@@ -1,14 +1,18 @@
+import functools
 import math
 
 import jax
 import jax.numpy as jnp
 from jax import lax
+from jax.experimental import pallas as pl
+from jax.experimental.pallas import tpu as pltpu
 from jax.sharding import PartitionSpec as P
 
 HD = 128
 BLOCK = 32
 GRID_H = 16
 GRID_W = 16
+MESH = pl.DeviceIdType.MESH
 
 
 def angles(positions):
@@ -137,9 +141,257 @@
     return restored[None]
 
 
+def fused_kernel(
+    nb,
+    nu,
+    q_ref,
+    k_ref,
+    v_ref,
+    ks_ref,
+    vs_ref,
+    pos_ref,
+    exp_ref,
+    step_ref,
+    gates_ref,
+    out_ref,
+    qkv_in,
+    send,
+    recv,
+    stale,
+    gates,
+    mixed,
+    in_sem,
+    own_sem,
+    fwd_send,
+    fwd_recv,
+    ret_send,
+    ret_recv,
+):
+    rows = q_ref.shape[1]
+    tokens = ks_ref.shape[1]
+    blocks = exp_ref.shape[2]
+    block = tokens // blocks
+    peers = nb * nu
+    own = send.shape[1]
+    width = own * HD
+    b = lax.axis_index("blk")
+    u = lax.axis_index("ulysses")
+    rank = u * nb + b
+    offsets = [(db, du) for db in range(nb) for du in range(nu) if (db, du) != (0, 0)]
+    offsets.sort(key=lambda pair: (-min(pair[0], nb - pair[0]), -pair[1]))
+
+    def ahead(db, du):
+        return lax.rem(b + db, nb), lax.rem(u + du, nu)
+
+    def behind(db, du):
+        return lax.rem(b + nb - db, nb), lax.rem(u + nu - du, nu)
+
+    def token_rows(bb, uu):
+        return pl.ds(pl.multiple_of((bb * nu + uu) * rows, rows), rows)
+
+    barrier = pltpu.get_barrier_semaphore()
+    for db, du in offsets:
+        bb, uu = ahead(db, du)
+        pl.semaphore_signal(
+            barrier, inc=1, device_id={"blk": bb, "ulysses": uu}, device_id_type=MESH
+        )
+
+    columns = pl.ds(pl.multiple_of(b * width, width), width)
+    loads = [
+        pltpu.make_async_copy(k_ref.at[0], qkv_in.at[1], in_sem.at[1]),
+        pltpu.make_async_copy(q_ref.at[0], qkv_in.at[0], in_sem.at[0]),
+        pltpu.make_async_copy(v_ref.at[0], qkv_in.at[2], in_sem.at[2]),
+        pltpu.make_async_copy(ks_ref.at[0, :, columns], stale.at[0], in_sem.at[3]),
+        pltpu.make_async_copy(vs_ref.at[0, :, columns], stale.at[1], in_sem.at[4]),
+        pltpu.make_async_copy(gates_ref.at[:, columns], gates, in_sem.at[5]),
+    ]
+    for load in loads:
+        load.start()
+
+    side = HD // 6
+    front = HD // 2 - 2 * side
+    lane = lax.broadcasted_iota(jnp.int32, (rows, HD), 1)
+    row = lax.broadcasted_iota(jnp.int32, (rows, HD), 0)
+    pair = lane >> 1
+    even = (lane & 1) == 0
+    position = jnp.zeros((rows, HD), jnp.int32)
+    for t in range(rows):
+        position = jnp.where(row == t, pos_ref[t], position)
+    in_front = pair < front
+    in_rows = pair < front + side
+    place = jnp.where(
+        in_front,
+        position // (GRID_H * GRID_W),
+        jnp.where(in_rows, position // GRID_W % GRID_H, position % GRID_W),
+    ).astype(jnp.float32)
+    within = jnp.where(in_front, pair, jnp.where(in_rows, pair - front, pair - front - side))
+    count = jnp.where(in_front, float(front), float(side))
+    phase = place * jnp.exp(-math.log(10000.0) * within.astype(jnp.float32) / count)
+    cosine = jnp.cos(phase)
+    sine = jnp.sin(phase)
+    sine = jnp.where(even, -sine, sine)
+
+    for load in loads[:3]:
+        load.wait()
+    for head in range(peers * own):
+        to, j = divmod(head, own)
+        at = slice(head * HD, (head + 1) * HD)
+        for which in range(2):
+            x = qkv_in[which, :, at].astype(jnp.float32)
+            other = jnp.where(even, pltpu.roll(x, HD - 1, 1), pltpu.roll(x, 1, 1))
+            send[to, j, which] = (x * cosine + other * sine).astype(jnp.bfloat16)
+        send[to, j, 2] = qkv_in[2, :, at]
+
+    pl.semaphore_wait(barrier, len(offsets))
+
+    forward = []
+    for j in range(own):
+        for i, (db, du) in enumerate(offsets):
+            bb, uu = ahead(db, du)
+            copy = pltpu.make_async_remote_copy(
+                src_ref=send.at[uu * nb + bb, j],
+                dst_ref=recv.at[j, :, token_rows(b, u)],
+                send_sem=fwd_send.at[j, i],
+                recv_sem=fwd_recv.at[j, i],
+                device_id={"blk": bb, "ulysses": uu},
+                device_id_type=MESH,
+            )
+            copy.start()
+            forward.append(copy)
+
+    for j in range(own):
+        recv[j, :, token_rows(b, u)] = send[rank, j]
+
+    for load in loads[3:]:
+        load.wait()
+    chosen = lax.broadcasted_iota(jnp.int32, gates.shape, 0) == step_ref[0]
+    gate_row = jnp.sum(
+        jnp.where(chosen, gates[...].astype(jnp.float32), 0.0), axis=0, keepdims=True
+    )
+
+    def residual(which, j):
+        at = slice(j * HD, (j + 1) * HD)
+        parts = []
+        for n in range(blocks):
+            span = slice(n * block, (n + 1) * block)
+            exponent = jnp.full((block, HD), exp_ref[which, 0, n, b * own + j], jnp.int32)
+            one = jnp.ones_like(exponent)
+            inverse = lax.shift_left(one, -exponent).astype(jnp.float32)
+            power = lax.shift_left(one, exponent + 16).astype(jnp.float32) * 2.0**-16
+            now = recv[j, 1 + which, span].astype(jnp.float32)
+            before = stale[which, span, at].astype(jnp.float32)
+            sent = jnp.clip((now - before) * inverse, -448.0, 448.0).astype(jnp.bfloat16)
+            parts.append((sent.astype(jnp.float32) * power).astype(jnp.bfloat16))
+        return jnp.concatenate(parts, axis=0)
+
+    back = []
+    for j in range(own):
+        for i, (db, du) in enumerate(offsets):
+            bb, uu = behind(db, du)
+            pltpu.make_async_remote_copy(
+                src_ref=send.at[rank, j],
+                dst_ref=recv.at[j, :, token_rows(bb, uu)],
+                send_sem=fwd_send.at[j, i],
+                recv_sem=fwd_recv.at[j, i],
+                device_id={"blk": bb, "ulysses": uu},
+                device_id_type=MESH,
+            ).wait_recv()
+        at = slice(j * HD, (j + 1) * HD)
+        query = recv[j, 0]
+        keys = jnp.concatenate([stale[0, :, at], residual(0, j)], axis=1)
+        scores = lax.dot_general(
+            jnp.concatenate([query, query], axis=1),
+            keys,
+            (((1,), (1,)), ((), ())),
+            preferred_element_type=jnp.float32,
+        ) * (1.0 / math.sqrt(HD))
+        peak = jnp.max(scores, axis=1, keepdims=True)
+        weights = jnp.exp(scores - peak).astype(jnp.bfloat16)
+        total = jnp.sum(weights.astype(jnp.float32), axis=1, keepdims=True)
+        values = jnp.concatenate([stale[1, :, at], residual(1, j)], axis=0)
+        sums = jnp.dot(
+            jnp.concatenate([weights, weights], axis=1),
+            values,
+            preferred_element_type=jnp.float32,
+        )
+        mixed[j] = (sums / total * gate_row[:, at]).astype(jnp.bfloat16)
+        target = pl.ds(pl.multiple_of((rank * own + j) * HD, HD), HD)
+        for i, (db, du) in enumerate(offsets):
+            bb, uu = ahead(db, du)
+            copy = pltpu.make_async_remote_copy(
+                src_ref=mixed.at[j, token_rows(bb, uu)],
+                dst_ref=out_ref.at[0, :, target],
+                send_sem=ret_send.at[j, i],
+                recv_sem=ret_recv.at[j, i],
+                device_id={"blk": bb, "ulysses": uu},
+                device_id_type=MESH,
+            )
+            copy.start()
+            back.append(copy)
+        out_ref[0, :, target] = mixed[j, token_rows(b, u)]
+
+    for copy in forward:
+        copy.wait_send()
+    for j in range(own):
+        for i, (db, du) in enumerate(offsets):
+            bb, uu = behind(db, du)
+            source = (uu * nb + bb) * own + j
+            pltpu.make_async_remote_copy(
+                src_ref=mixed.at[j, token_rows(b, u)],
+                dst_ref=out_ref.at[0, :, pl.ds(pl.multiple_of(source * HD, HD), HD)],
+                send_sem=ret_send.at[j, i],
+                recv_sem=ret_recv.at[j, i],
+                device_id={"blk": bb, "ulysses": uu},
+                device_id_type=MESH,
+            ).wait_recv()
+    for copy in back:
+        copy.wait_send()
+
+
+def fused(nb, nu, *args):
+    queries, key_stale, step_gates = args[0], args[3], args[8]
+    rows, features = queries.shape[1:]
+    tokens, columns = key_stale.shape[1:]
+    own = columns // HD // nb
+    width = own * HD
+    peers = nb * nu
+    hbm = pl.BlockSpec(memory_space=pl.ANY)
+    smem = pl.BlockSpec(memory_space=pltpu.SMEM)
+    pairs = pltpu.SemaphoreType.DMA((own, peers - 1))
+    return pl.pallas_call(
+        functools.partial(fused_kernel, nb, nu),
+        out_shape=jax.ShapeDtypeStruct(queries.shape, jnp.bfloat16),
+        in_specs=[hbm] * 5 + [smem] * 3 + [hbm],
+        out_specs=pl.BlockSpec(memory_space=pltpu.VMEM),
+        scratch_shapes=[
+            pltpu.VMEM((3, rows, features), jnp.bfloat16),
+            pltpu.VMEM((peers, own, 3, rows, HD), jnp.bfloat16),
+            pltpu.VMEM((own, 3, tokens, HD), jnp.bfloat16),
+            pltpu.VMEM((2, tokens, width), jnp.bfloat16),
+            pltpu.VMEM((step_gates.shape[0], width), jnp.bfloat16),
+            pltpu.VMEM((own, tokens, HD), jnp.bfloat16),
+            pltpu.SemaphoreType.DMA((6,)),
+            pltpu.SemaphoreType.DMA,
+            pairs,
+            pairs,
+            pairs,
+            pairs,
+        ],
+        compiler_params=pltpu.CompilerParams(collective_id=0, has_side_effects=True),
+    )(*args)
+
+
 def solution(mesh):
+    nb, nu = mesh.shape["blk"], mesh.shape["ulysses"]
+
+    def body(*args):
+        heads = args[3].shape[2] // HD
+        if heads % nb == 0 and nb * nu > 1:
+            return fused(nb, nu, *args)
+        return shards(*args)
+
     return jax.shard_map(
-        shards,
+        body,
         mesh=mesh,
         in_specs=(
             P("cfg", ("groups", "blk", "ulysses"), None),

time: 71 us -> 22.7 us (0.32)
  blocking collectives: 36.5 us -> 0 us
  Pallas kernels: 0 us -> 20.9 us
  starting transfers between devices: 11 us -> 0 us
  other arithmetic: 10.7 us -> 0 us
  local copies, waits for them, and re-layouts: 6.7 us -> 1.54 us
  waiting for transfers between devices: 3.9 us -> 0 us
  matrix products: 1.18 us -> 0 us
    all_gather x2 -> x0, blocking collectives: 29.9 us -> none  [the longest x1 15.2 us: shards(): lax.all_gather(key_sent, 'blk', axis=0, tiled=True)]
    pallas_call x0 -> x1, Pallas kernels: none -> 20.9 us  [fused(): pl.pallas_call(functools.partial(fused_kernel, nb, nu), out_shape=jax.Sha...]
    all_to_all x3 -> x0, starting transfers between devices: 11 us -> none  [the longest x1 4.34 us: shards(): lax.all_to_all(key_turned, 'ulysses', split_axis=1, concat_axis=0, tiled=...]
    another operation x2 -> x0, other arithmetic: 8.51 us -> none
    all_to_all x1 -> x0, blocking collectives: 6.65 us -> none  [shards(): lax.all_to_all(gated.reshape(tok_rows, feature_width), 'ulysses', split_a...]
    all_to_all x3 -> x0, waiting for transfers between devices: 3.9 us -> none  [the longest x1 3.15 us: shards(): lax.all_to_all(value_now[0], 'ulysses', split_axis=1, concat_axis=0, tile...]
    convert_element_type x7 -> x0, local copies, waits for them, and re-layouts: 3.61 us -> none  [the longest x2 1.44 us: rotate(): source.astype(jnp.float32).reshape(leading + (head_count, HD // 2, 2))]
    convert_element_type x4 -> x0, other arithmetic: 1.66 us -> none  [the longest x1 0.77 us: shards(): lax.dynamic_index_in_dim(step_gates, step_index[0], 0, keepdims=False)]
  transfers between devices with their start and end apart: 3 -> 0, of which waited for: 2 -> 0; matrix products, arithmetic and copies ran while one was open for 7% -> 0% of each run, Pallas kernels for 0% -> 0%
where the time goes in v1:
time: 22.7 us; the launch traced here: 22.5 us
  Pallas kernels  20.9 us (92%)
  local copies, waits for them, and re-layouts  1.54 us (7%)
    pallas_call x1, Pallas kernels, fused(): pl.pallas_call(functools.partial(fused_kernel, nb, nu), out_shape=jax.Sha...  20.9 us
    unnamed x1, local copies, waits for them, and re-layouts  1.54 us

profile of v1, /device:TPU:0, one launch (start us, length us, event | category | flops | bytes accessed | tf_op | source)
XLA Modules:
  0.0 22.5 jit_solution(1269273252998588132)
XLA Ops:
  0.0 20.9 %shard_map.91 = bf16[1,16,3072]{2,1,0:T(8,128)(2,1)} custom-call(bf16[1,16,3072]{2,1,0:T(8,128)(2,1)} %q_ref.1, bf16[1,16,3072]{2,1,0:T(8,128)(2,1)} %k_ref.1, bf16[1,16,3072]{2,1,0:T(8,128)(2,1)} %v_ref.1, bf16[1,128,1536]{2,1,0:T(8,128)(2,1)} %ks_ref.1, bf16[1,128,1536]{2,1,0:T(8,128)(2,1)} %vs_ref.1, s32[16]{0:T(128)} %pos_ref.1, ...), custom_call_target="tpu_custom_call" | custom-call | tf_op jit(solution)/shard_map/pallas_call | solution.py:361
  20.9 1.5 %copy.11 = bf16[1,16,3072]{2,1,0:T(8,128)(2,1)} copy(bf16[1,16,3072]{2,1,0:T(8,128)(2,1)} %shard_map.91) | data formatting | bytes 196608

commit v2 on v1

--- a/solution.py
+++ b/solution.py
@@ -149,9 +149,9 @@
     v_ref,
     ks_ref,
     vs_ref,
-    pos_ref,
-    exp_ref,
-    step_ref,
+    pos_hbm,
+    exp_hbm,
+    step_hbm,
     gates_ref,
     out_ref,
     qkv_in,
@@ -160,8 +160,10 @@
     stale,
     gates,
     mixed,
+    pos_ref,
+    exp_ref,
+    step_ref,
     in_sem,
-    own_sem,
     fwd_send,
     fwd_recv,
     ret_send,
@@ -171,12 +173,12 @@
     tokens = ks_ref.shape[1]
     blocks = exp_ref.shape[2]
     block = tokens // blocks
-    peers = nb * nu
     own = send.shape[1]
     width = own * HD
     b = lax.axis_index("blk")
     u = lax.axis_index("ulysses")
     rank = u * nb + b
+    place_of = b * nu + u
     offsets = [(db, du) for db in range(nb) for du in range(nu) if (db, du) != (0, 0)]
     offsets.sort(key=lambda pair: (-min(pair[0], nb - pair[0]), -pair[1]))
 
@@ -188,6 +190,9 @@
 
     def token_rows(bb, uu):
         return pl.ds(pl.multiple_of((bb * nu + uu) * rows, rows), rows)
+
+    def head_columns(of_rank):
+        return pl.ds(pl.multiple_of(of_rank * width, width), width)
 
     barrier = pltpu.get_barrier_semaphore()
     for db, du in offsets:
@@ -196,14 +201,17 @@
             barrier, inc=1, device_id={"blk": bb, "ulysses": uu}, device_id_type=MESH
         )
 
-    columns = pl.ds(pl.multiple_of(b * width, width), width)
+    columns = head_columns(b)
     loads = [
-        pltpu.make_async_copy(k_ref.at[0], qkv_in.at[1], in_sem.at[1]),
-        pltpu.make_async_copy(q_ref.at[0], qkv_in.at[0], in_sem.at[0]),
-        pltpu.make_async_copy(v_ref.at[0], qkv_in.at[2], in_sem.at[2]),
-        pltpu.make_async_copy(ks_ref.at[0, :, columns], stale.at[0], in_sem.at[3]),
-        pltpu.make_async_copy(vs_ref.at[0, :, columns], stale.at[1], in_sem.at[4]),
-        pltpu.make_async_copy(gates_ref.at[:, columns], gates, in_sem.at[5]),
+        pltpu.make_async_copy(pos_hbm, pos_ref, in_sem.at[0]),
+        pltpu.make_async_copy(q_ref.at[0], qkv_in.at[0], in_sem.at[1]),
+        pltpu.make_async_copy(k_ref.at[0], qkv_in.at[1], in_sem.at[2]),
+        pltpu.make_async_copy(v_ref.at[0], qkv_in.at[2], in_sem.at[3]),
+        pltpu.make_async_copy(exp_hbm, exp_ref, in_sem.at[4]),
+        pltpu.make_async_copy(step_hbm, step_ref, in_sem.at[5]),
+        pltpu.make_async_copy(ks_ref.at[0, :, columns], stale.at[0], in_sem.at[6]),
+        pltpu.make_async_copy(vs_ref.at[0, :, columns], stale.at[1], in_sem.at[7]),
+        pltpu.make_async_copy(gates_ref.at[:, columns], gates, in_sem.at[8]),
     ]
     for load in loads:
         load.start()
@@ -214,55 +222,60 @@
     row = lax.broadcasted_iota(jnp.int32, (rows, HD), 0)
     pair = lane >> 1
     even = (lane & 1) == 0
+    in_front = pair < front
+    in_rows = pair < front + side
+    within = jnp.where(in_front, pair, jnp.where(in_rows, pair - front, pair - front - side))
+    count = jnp.where(in_front, float(front), float(side))
+    frequency = jnp.exp(-math.log(10000.0) * within.astype(jnp.float32) / count)
+    loads[0].wait()
     position = jnp.zeros((rows, HD), jnp.int32)
     for t in range(rows):
         position = jnp.where(row == t, pos_ref[t], position)
-    in_front = pair < front
-    in_rows = pair < front + side
     place = jnp.where(
         in_front,
         position // (GRID_H * GRID_W),
         jnp.where(in_rows, position // GRID_W % GRID_H, position % GRID_W),
     ).astype(jnp.float32)
-    within = jnp.where(in_front, pair, jnp.where(in_rows, pair - front, pair - front - side))
-    count = jnp.where(in_front, float(front), float(side))
-    phase = place * jnp.exp(-math.log(10000.0) * within.astype(jnp.float32) / count)
+    phase = place * frequency
     cosine = jnp.cos(phase)
     sine = jnp.sin(phase)
     sine = jnp.where(even, -sine, sine)
 
-    for load in loads[:3]:
+    for load in loads[1:4]:
         load.wait()
-    for head in range(peers * own):
-        to, j = divmod(head, own)
-        at = slice(head * HD, (head + 1) * HD)
-        for which in range(2):
-            x = qkv_in[which, :, at].astype(jnp.float32)
-            other = jnp.where(even, pltpu.roll(x, HD - 1, 1), pltpu.roll(x, 1, 1))
-            send[to, j, which] = (x * cosine + other * sine).astype(jnp.bfloat16)
-        send[to, j, 2] = qkv_in[2, :, at]
-
-    pl.semaphore_wait(barrier, len(offsets))
-
-    forward = []
-    for j in range(own):
-        for i, (db, du) in enumerate(offsets):
-            bb, uu = ahead(db, du)
-            copy = pltpu.make_async_remote_copy(
-                src_ref=send.at[uu * nb + bb, j],
-                dst_ref=recv.at[j, :, token_rows(b, u)],
-                send_sem=fwd_send.at[j, i],
-                recv_sem=fwd_recv.at[j, i],
-                device_id={"blk": bb, "ulysses": uu},
-                device_id_type=MESH,
-            )
-            copy.start()
-            forward.append(copy)
-
-    for j in range(own):
-        recv[j, :, token_rows(b, u)] = send[rank, j]
-
-    for load in loads[3:]:
+
+    def turned(which, head):
+        x = qkv_in[which, :, pl.ds(pl.multiple_of(head * HD, HD), HD)].astype(jnp.float32)
+        other = jnp.where(even, pltpu.roll(x, HD - 1, 1), pltpu.roll(x, 1, 1))
+        return (x * cosine + other * sine).astype(jnp.bfloat16)
+
+    def fill(target, to_rank):
+        for j in range(own):
+            head = to_rank * own + j
+            target[j, 0] = turned(0, head)
+            target[j, 1] = turned(1, head)
+            target[j, 2] = qkv_in[2, :, pl.ds(pl.multiple_of(head * HD, HD), HD)]
+
+    def forward(i, db, du):
+        bb, uu = ahead(db, du)
+        return pltpu.make_async_remote_copy(
+            src_ref=send.at[i],
+            dst_ref=recv.at[place_of],
+            send_sem=fwd_send.at[i],
+            recv_sem=fwd_recv.at[i],
+            device_id={"blk": bb, "ulysses": uu},
+            device_id_type=MESH,
+        )
+
+    for i, (db, du) in enumerate(offsets):
+        bb, uu = ahead(db, du)
+        fill(send.at[i], uu * nb + bb)
+        if i == 0:
+            pl.semaphore_wait(barrier, len(offsets))
+        forward(i, db, du).start()
+    fill(recv.at[place_of], rank)
+
+    for load in loads[4:]:
         load.wait()
     chosen = lax.broadcasted_iota(jnp.int32, gates.shape, 0) == step_ref[0]
     gate_row = jnp.sum(
@@ -272,32 +285,35 @@
     def residual(which, j):
         at = slice(j * HD, (j + 1) * HD)
         parts = []
+        per = block // rows
         for n in range(blocks):
             span = slice(n * block, (n + 1) * block)
             exponent = jnp.full((block, HD), exp_ref[which, 0, n, b * own + j], jnp.int32)
             one = jnp.ones_like(exponent)
             inverse = lax.shift_left(one, -exponent).astype(jnp.float32)
             power = lax.shift_left(one, exponent + 16).astype(jnp.float32) * 2.0**-16
-            now = recv[j, 1 + which, span].astype(jnp.float32)
+            now = jnp.concatenate(
+                [recv[n * per + m, j, 1 + which] for m in range(per)], axis=0
+            ).astype(jnp.float32)
             before = stale[which, span, at].astype(jnp.float32)
             sent = jnp.clip((now - before) * inverse, -448.0, 448.0).astype(jnp.bfloat16)
             parts.append((sent.astype(jnp.float32) * power).astype(jnp.bfloat16))
         return jnp.concatenate(parts, axis=0)
 
-    back = []
+    for i, (db, du) in enumerate(offsets):
+        bb, uu = behind(db, du)
+        pltpu.make_async_remote_copy(
+            src_ref=send.at[i],
+            dst_ref=recv.at[bb * nu + uu],
+            send_sem=fwd_send.at[i],
+            recv_sem=fwd_recv.at[i],
+            device_id={"blk": bb, "ulysses": uu},
+            device_id_type=MESH,
+        ).wait_recv()
+
     for j in range(own):
-        for i, (db, du) in enumerate(offsets):
-            bb, uu = behind(db, du)
-            pltpu.make_async_remote_copy(
-                src_ref=send.at[rank, j],
-                dst_ref=recv.at[j, :, token_rows(bb, uu)],
-                send_sem=fwd_send.at[j, i],
-                recv_sem=fwd_recv.at[j, i],
-                device_id={"blk": bb, "ulysses": uu},
-                device_id_type=MESH,
-            ).wait_recv()
         at = slice(j * HD, (j + 1) * HD)
-        query = recv[j, 0]
+        query = jnp.concatenate([recv[t, j, 0] for t in range(nb * nu)], axis=0)
         keys = jnp.concatenate([stale[0, :, at], residual(0, j)], axis=1)
         scores = lax.dot_general(
             jnp.concatenate([query, query], axis=1),
@@ -314,64 +330,67 @@
             values,
             preferred_element_type=jnp.float32,
         )
-        mixed[j] = (sums / total * gate_row[:, at]).astype(jnp.bfloat16)
-        target = pl.ds(pl.multiple_of((rank * own + j) * HD, HD), HD)
-        for i, (db, du) in enumerate(offsets):
-            bb, uu = ahead(db, du)
-            copy = pltpu.make_async_remote_copy(
-                src_ref=mixed.at[j, token_rows(bb, uu)],
-                dst_ref=out_ref.at[0, :, target],
-                send_sem=ret_send.at[j, i],
-                recv_sem=ret_recv.at[j, i],
-                device_id={"blk": bb, "ulysses": uu},
-                device_id_type=MESH,
-            )
-            copy.start()
-            back.append(copy)
-        out_ref[0, :, target] = mixed[j, token_rows(b, u)]
-
-    for copy in forward:
-        copy.wait_send()
-    for j in range(own):
-        for i, (db, du) in enumerate(offsets):
-            bb, uu = behind(db, du)
-            source = (uu * nb + bb) * own + j
-            pltpu.make_async_remote_copy(
-                src_ref=mixed.at[j, token_rows(b, u)],
-                dst_ref=out_ref.at[0, :, pl.ds(pl.multiple_of(source * HD, HD), HD)],
-                send_sem=ret_send.at[j, i],
-                recv_sem=ret_recv.at[j, i],
-                device_id={"blk": bb, "ulysses": uu},
-                device_id_type=MESH,
-            ).wait_recv()
-    for copy in back:
-        copy.wait_send()
+        mixed[:, at] = (sums / total * gate_row[:, at]).astype(jnp.bfloat16)
+
+    def back(i, db, du):
+        bb, uu = ahead(db, du)
+        return pltpu.make_async_remote_copy(
+            src_ref=mixed.at[token_rows(bb, uu)],
+            dst_ref=out_ref.at[0, :, head_columns(rank)],
+            send_sem=ret_send.at[i],
+            recv_sem=ret_recv.at[i],
+            device_id={"blk": bb, "ulysses": uu},
+            device_id_type=MESH,
+        )
+
+    for i, (db, du) in enumerate(offsets):
+        back(i, db, du).start()
+    out_ref[0, :, head_columns(rank)] = mixed[token_rows(b, u)]
+    for i, (db, du) in enumerate(offsets):
+        forward(i, db, du).wait_send()
+    for i, (db, du) in enumerate(offsets):
+        bb, uu = behind(db, du)
+        pltpu.make_async_remote_copy(
+            src_ref=mixed.at[token_rows(b, u)],
+            dst_ref=out_ref.at[0, :, head_columns(uu * nb + bb)],
+            send_sem=ret_send.at[i],
+            recv_sem=ret_recv.at[i],
+            device_id={"blk": bb, "ulysses": uu},
+            device_id_type=MESH,
+        ).wait_recv()
+    for i, (db, du) in enumerate(offsets):
+        back(i, db, du).wait_send()
 
 
 def fused(nb, nu, *args):
-    queries, key_stale, step_gates = args[0], args[3], args[8]
+    queries, key_stale, positions, exponents, step_index, step_gates = (
+        args[0],
+        args[3],
+        *args[5:],
+    )
     rows, features = queries.shape[1:]
     tokens, columns = key_stale.shape[1:]
     own = columns // HD // nb
     width = own * HD
     peers = nb * nu
     hbm = pl.BlockSpec(memory_space=pl.ANY)
-    smem = pl.BlockSpec(memory_space=pltpu.SMEM)
-    pairs = pltpu.SemaphoreType.DMA((own, peers - 1))
+    pairs = pltpu.SemaphoreType.DMA((peers - 1,))
     return pl.pallas_call(
         functools.partial(fused_kernel, nb, nu),
         out_shape=jax.ShapeDtypeStruct(queries.shape, jnp.bfloat16),
-        in_specs=[hbm] * 5 + [smem] * 3 + [hbm],
+        in_specs=[hbm] * 9,
         out_specs=pl.BlockSpec(memory_space=pltpu.VMEM),
         scratch_shapes=[
             pltpu.VMEM((3, rows, features), jnp.bfloat16),
+            pltpu.VMEM((peers - 1, own, 3, rows, HD), jnp.bfloat16),
             pltpu.VMEM((peers, own, 3, rows, HD), jnp.bfloat16),
-            pltpu.VMEM((own, 3, tokens, HD), jnp.bfloat16),
             pltpu.VMEM((2, tokens, width), jnp.bfloat16),
             pltpu.VMEM((step_gates.shape[0], width), jnp.bfloat16),
-            pltpu.VMEM((own, tokens, HD), jnp.bfloat16),
-            pltpu.SemaphoreType.DMA((6,)),
-            pltpu.SemaphoreType.DMA,
+            pltpu.VMEM((tokens, width), jnp.bfloat16),
+            pltpu.SMEM(positions.shape, jnp.int32),
+            pltpu.SMEM(exponents.shape, jnp.int32),
+            pltpu.SMEM(step_index.shape, jnp.int32),
+            pltpu.SemaphoreType.DMA((9,)),
             pairs,
             pairs,
             pairs,

time: 22.7 us -> 20.5 us (0.903)
  Pallas kernels: 20.9 us -> 18.8 us
    pallas_call x1, Pallas kernels: 20.9 us -> 18.8 us  [fused(): pl.pallas_call(functools.partial(fused_kernel, nb, nu), out_shape=jax.Sha...]
where the time goes in v2:
time: 20.5 us; the launch traced here: 20.3 us
  Pallas kernels  18.8 us (92%)
  local copies, waits for them, and re-layouts  1.54 us (8%)
    pallas_call x1, Pallas kernels, fused(): pl.pallas_call(functools.partial(fused_kernel, nb, nu), out_shape=jax.Sha...  18.8 us
    unnamed x1, local copies, waits for them, and re-layouts  1.54 us

profile of v2, /device:TPU:0, one launch (start us, length us, event | category | flops | bytes accessed | tf_op | source)
XLA Modules:
  0.0 20.3 jit_solution(9566168605877205914)
XLA Ops:
  0.0 18.8 %shard_map.91 = bf16[1,16,3072]{2,1,0:T(8,128)(2,1)} custom-call(bf16[1,16,3072]{2,1,0:T(8,128)(2,1)} %q_ref.1, bf16[1,16,3072]{2,1,0:T(8,128)(2,1)} %k_ref.1, bf16[1,16,3072]{2,1,0:T(8,128)(2,1)} %v_ref.1, bf16[1,128,1536]{2,1,0:T(8,128)(2,1)} %ks_ref.1, bf16[1,128,1536]{2,1,0:T(8,128)(2,1)} %vs_ref.1, s32[16]{0:T(128)} %pos_hbm.1, ...), custom_call_target="tpu_custom_call" | custom-call | tf_op jit(solution)/shard_map/pallas_call | solution.py:378
  18.8 1.5 %copy.11 = bf16[1,16,3072]{2,1,0:T(8,128)(2,1)} copy(bf16[1,16,3072]{2,1,0:T(8,128)(2,1)} %shard_map.91) | data formatting | bytes 196608

commit v3 on v2

--- a/solution.py
+++ b/solution.py
@@ -345,7 +345,10 @@
 
     for i, (db, du) in enumerate(offsets):
         back(i, db, du).start()
-    out_ref[0, :, head_columns(rank)] = mixed[token_rows(b, u)]
+    kept = pltpu.make_async_copy(
+        mixed.at[token_rows(b, u)], out_ref.at[0, :, head_columns(rank)], in_sem.at[9]
+    )
+    kept.start()
     for i, (db, du) in enumerate(offsets):
         forward(i, db, du).wait_send()
     for i, (db, du) in enumerate(offsets):
@@ -360,6 +363,7 @@
         ).wait_recv()
     for i, (db, du) in enumerate(offsets):
         back(i, db, du).wait_send()
+    kept.wait()
 
 
 def fused(nb, nu, *args):
@@ -379,7 +383,7 @@
         functools.partial(fused_kernel, nb, nu),
         out_shape=jax.ShapeDtypeStruct(queries.shape, jnp.bfloat16),
         in_specs=[hbm] * 9,
-        out_specs=pl.BlockSpec(memory_space=pltpu.VMEM),
+        out_specs=hbm,
         scratch_shapes=[
             pltpu.VMEM((3, rows, features), jnp.bfloat16),
             pltpu.VMEM((peers - 1, own, 3, rows, HD), jnp.bfloat16),
@@ -390,7 +394,7 @@
             pltpu.SMEM(positions.shape, jnp.int32),
             pltpu.SMEM(exponents.shape, jnp.int32),
             pltpu.SMEM(step_index.shape, jnp.int32),
-            pltpu.SemaphoreType.DMA((9,)),
+            pltpu.SemaphoreType.DMA((10,)),
             pairs,
             pairs,
             pairs,
@@ -405,7 +409,8 @@
 
     def body(*args):
         heads = args[3].shape[2] // HD
-        if heads % nb == 0 and nb * nu > 1:
+        block = args[3].shape[1] // args[6].shape[2]
+        if heads % nb == 0 and nb * nu > 1 and block % args[0].shape[1] == 0:
             return fused(nb, nu, *args)
         return shards(*args)
 

time: 20.5 us -> 20 us (0.976)
  Pallas kernels: 18.8 us -> 18.3 us
    pallas_call x1, Pallas kernels: 18.8 us -> 18.3 us  [fused(): pl.pallas_call(functools.partial(fused_kernel, nb, nu), out_shape=jax.Sha...]
where the time goes in v3:
time: 20 us; the launch traced here: 19.8 us
  Pallas kernels  18.3 us (92%)
  local copies, waits for them, and re-layouts  1.54 us (8%)
    pallas_call x1, Pallas kernels, fused(): pl.pallas_call(functools.partial(fused_kernel, nb, nu), out_shape=jax.Sha...  18.3 us
    unnamed x1, local copies, waits for them, and re-layouts  1.54 us

profile of v3, /device:TPU:0, one launch (start us, length us, event | category | flops | bytes accessed | tf_op | source)
XLA Modules:
  0.0 19.8 jit_solution(4810648011122873949)
XLA Ops:
  0.0 18.3 %shard_map.91 = bf16[1,16,3072]{2,1,0:T(8,128)(2,1)} custom-call(bf16[1,16,3072]{2,1,0:T(8,128)(2,1)} %q_ref.1, bf16[1,16,3072]{2,1,0:T(8,128)(2,1)} %k_ref.1, bf16[1,16,3072]{2,1,0:T(8,128)(2,1)} %v_ref.1, bf16[1,128,1536]{2,1,0:T(8,128)(2,1)} %ks_ref.1, bf16[1,128,1536]{2,1,0:T(8,128)(2,1)} %vs_ref.1, s32[16]{0:T(128)} %pos_hbm.1, ...), custom_call_target="tpu_custom_call" | custom-call | tf_op jit(solution)/shard_map/pallas_call | solution.py:382
  18.3 1.5 %copy.11 = bf16[1,16,3072]{2,1,0:T(8,128)(2,1)} copy(bf16[1,16,3072]{2,1,0:T(8,128)(2,1)} %shard_map.91) | data formatting | bytes 196608

commit v4 on v3

--- a/solution.py
+++ b/solution.py
@@ -213,7 +213,7 @@
         pltpu.make_async_copy(vs_ref.at[0, :, columns], stale.at[1], in_sem.at[7]),
         pltpu.make_async_copy(gates_ref.at[:, columns], gates, in_sem.at[8]),
     ]
-    for load in loads:
+    for load in loads[:4]:
         load.start()
 
     side = HD // 6
@@ -273,6 +273,8 @@
         if i == 0:
             pl.semaphore_wait(barrier, len(offsets))
         forward(i, db, du).start()
+    for load in loads[4:]:
+        load.start()
     fill(recv.at[place_of], rank)
 
     for load in loads[4:]:
@@ -350,8 +352,6 @@
     )
     kept.start()
     for i, (db, du) in enumerate(offsets):
-        forward(i, db, du).wait_send()
-    for i, (db, du) in enumerate(offsets):
         bb, uu = behind(db, du)
         pltpu.make_async_remote_copy(
             src_ref=mixed.at[token_rows(b, u)],
@@ -363,6 +363,7 @@
         ).wait_recv()
     for i, (db, du) in enumerate(offsets):
         back(i, db, du).wait_send()
+        forward(i, db, du).wait_send()
     kept.wait()
 
 

time: 20 us -> 20 us (level)
  no operation moved by 1% of the time
where the time goes in v4:
time: 20 us; the launch traced here: 19.8 us
  Pallas kernels  18.3 us (92%)
  local copies, waits for them, and re-layouts  1.54 us (8%)
    pallas_call x1, Pallas kernels, fused(): pl.pallas_call(functools.partial(fused_kernel, nb, nu), out_shape=jax.Sha...  18.3 us
    unnamed x1, local copies, waits for them, and re-layouts  1.54 us

profile of v4, /device:TPU:0, one launch (start us, length us, event | category | flops | bytes accessed | tf_op | source)
XLA Modules:
  0.0 19.8 jit_solution(2368161488347358720)
XLA Ops:
  0.0 18.3 %shard_map.91 = bf16[1,16,3072]{2,1,0:T(8,128)(2,1)} custom-call(bf16[1,16,3072]{2,1,0:T(8,128)(2,1)} %q_ref.1, bf16[1,16,3072]{2,1,0:T(8,128)(2,1)} %k_ref.1, bf16[1,16,3072]{2,1,0:T(8,128)(2,1)} %v_ref.1, bf16[1,128,1536]{2,1,0:T(8,128)(2,1)} %ks_ref.1, bf16[1,128,1536]{2,1,0:T(8,128)(2,1)} %vs_ref.1, s32[16]{0:T(128)} %pos_hbm.1, ...), custom_call_target="tpu_custom_call" | custom-call | tf_op jit(solution)/shard_map/pallas_call | solution.py:383
  18.3 1.5 %copy.11 = bf16[1,16,3072]{2,1,0:T(8,128)(2,1)} copy(bf16[1,16,3072]{2,1,0:T(8,128)(2,1)} %shard_map.91) | data formatting | bytes 196608

commit v5 on v4

--- a/solution.py
+++ b/solution.py
@@ -158,6 +158,7 @@
     send,
     recv,
     stale,
+    fresh,
     gates,
     mixed,
     pos_ref,
@@ -284,25 +285,26 @@
         jnp.where(chosen, gates[...].astype(jnp.float32), 0.0), axis=0, keepdims=True
     )
 
-    def residual(which, j):
-        at = slice(j * HD, (j + 1) * HD)
-        parts = []
-        per = block // rows
-        for n in range(blocks):
-            span = slice(n * block, (n + 1) * block)
-            exponent = jnp.full((block, HD), exp_ref[which, 0, n, b * own + j], jnp.int32)
-            one = jnp.ones_like(exponent)
-            inverse = lax.shift_left(one, -exponent).astype(jnp.float32)
-            power = lax.shift_left(one, exponent + 16).astype(jnp.float32) * 2.0**-16
-            now = jnp.concatenate(
-                [recv[n * per + m, j, 1 + which] for m in range(per)], axis=0
-            ).astype(jnp.float32)
-            before = stale[which, span, at].astype(jnp.float32)
-            sent = jnp.clip((now - before) * inverse, -448.0, 448.0).astype(jnp.bfloat16)
-            parts.append((sent.astype(jnp.float32) * power).astype(jnp.bfloat16))
-        return jnp.concatenate(parts, axis=0)
-
-    for i, (db, du) in enumerate(offsets):
+    def encode(bb):
+        span = pl.ds(pl.multiple_of(bb * nu * rows, nu * rows), nu * rows)
+        block_of = bb * nu * rows // block
+        for which in range(2):
+            for j in range(own):
+                at = slice(j * HD, (j + 1) * HD)
+                exponent = jnp.full(
+                    (nu * rows, HD), exp_ref[which, 0, block_of, b * own + j], jnp.int32
+                )
+                one = jnp.ones_like(exponent)
+                inverse = lax.shift_left(one, -exponent).astype(jnp.float32)
+                power = lax.shift_left(one, exponent + 16).astype(jnp.float32) * 2.0**-16
+                now = jnp.concatenate(
+                    [recv[bb * nu + m, j, 1 + which] for m in range(nu)], axis=0
+                ).astype(jnp.float32)
+                before = stale[which, span, at].astype(jnp.float32)
+                sent = jnp.clip((now - before) * inverse, -448.0, 448.0).astype(jnp.bfloat16)
+                fresh[which, span, at] = (sent.astype(jnp.float32) * power).astype(jnp.bfloat16)
+
+    def arrived(i, db, du):
         bb, uu = behind(db, du)
         pltpu.make_async_remote_copy(
             src_ref=send.at[i],
@@ -313,10 +315,16 @@
             device_id_type=MESH,
         ).wait_recv()
 
+    for distance in sorted(range(nb), key=lambda d: -min(d, nb - d) if d else -nb):
+        for i, (db, du) in enumerate(offsets):
+            if db == distance:
+                arrived(i, db, du)
+        encode(lax.rem(b + nb - distance, nb))
+
     for j in range(own):
         at = slice(j * HD, (j + 1) * HD)
         query = jnp.concatenate([recv[t, j, 0] for t in range(nb * nu)], axis=0)
-        keys = jnp.concatenate([stale[0, :, at], residual(0, j)], axis=1)
+        keys = jnp.concatenate([stale[0, :, at], fresh[0, :, at]], axis=1)
         scores = lax.dot_general(
             jnp.concatenate([query, query], axis=1),
             keys,
@@ -326,7 +334,7 @@
         peak = jnp.max(scores, axis=1, keepdims=True)
         weights = jnp.exp(scores - peak).astype(jnp.bfloat16)
         total = jnp.sum(weights.astype(jnp.float32), axis=1, keepdims=True)
-        values = jnp.concatenate([stale[1, :, at], residual(1, j)], axis=0)
+        values = jnp.concatenate([stale[1, :, at], fresh[1, :, at]], axis=0)
         sums = jnp.dot(
             jnp.concatenate([weights, weights], axis=1),
             values,
@@ -351,6 +359,8 @@
         mixed.at[token_rows(b, u)], out_ref.at[0, :, head_columns(rank)], in_sem.at[9]
     )
     kept.start()
+    for i, (db, du) in enumerate(offsets):
+        forward(i, db, du).wait_send()
     for i, (db, du) in enumerate(offsets):
         bb, uu = behind(db, du)
         pltpu.make_async_remote_copy(
@@ -363,7 +373,6 @@
         ).wait_recv()
     for i, (db, du) in enumerate(offsets):
         back(i, db, du).wait_send()
-        forward(i, db, du).wait_send()
     kept.wait()
 
 
@@ -390,6 +399,7 @@
             pltpu.VMEM((peers - 1, own, 3, rows, HD), jnp.bfloat16),
             pltpu.VMEM((peers, own, 3, rows, HD), jnp.bfloat16),
             pltpu.VMEM((2, tokens, width), jnp.bfloat16),
+            pltpu.VMEM((2, tokens, width), jnp.bfloat16),
             pltpu.VMEM((step_gates.shape[0], width), jnp.bfloat16),
             pltpu.VMEM((tokens, width), jnp.bfloat16),
             pltpu.SMEM(positions.shape, jnp.int32),
@@ -411,7 +421,7 @@
     def body(*args):
         heads = args[3].shape[2] // HD
         block = args[3].shape[1] // args[6].shape[2]
-        if heads % nb == 0 and nb * nu > 1 and block % args[0].shape[1] == 0:
+        if heads % nb == 0 and nb * nu > 1 and block % (args[0].shape[1] * nu) == 0:
             return fused(nb, nu, *args)
         return shards(*args)
 

time: 20 us -> 20 us (level)
  no operation moved by 1% of the time
where the time goes in v5:
time: 20 us; the launch traced here: 19.8 us
  Pallas kernels  18.3 us (92%)
  local copies, waits for them, and re-layouts  1.54 us (8%)
    pallas_call x1, Pallas kernels, fused(): pl.pallas_call(functools.partial(fused_kernel, nb, nu), out_shape=jax.Sha...  18.3 us
    unnamed x1, local copies, waits for them, and re-layouts  1.54 us

profile of v5, /device:TPU:0, one launch (start us, length us, event | category | flops | bytes accessed | tf_op | source)
XLA Modules:
  0.0 19.8 jit_solution(7791604089431908622)
XLA Ops:
  0.0 18.3 %shard_map.91 = bf16[1,16,3072]{2,1,0:T(8,128)(2,1)} custom-call(bf16[1,16,3072]{2,1,0:T(8,128)(2,1)} %q_ref.1, bf16[1,16,3072]{2,1,0:T(8,128)(2,1)} %k_ref.1, bf16[1,16,3072]{2,1,0:T(8,128)(2,1)} %v_ref.1, bf16[1,128,1536]{2,1,0:T(8,128)(2,1)} %ks_ref.1, bf16[1,128,1536]{2,1,0:T(8,128)(2,1)} %vs_ref.1, s32[16]{0:T(128)} %pos_hbm.1, ...), custom_call_target="tpu_custom_call" | custom-call | tf_op jit(solution)/shard_map/pallas_call | solution.py:392
  18.3 1.5 %copy.11 = bf16[1,16,3072]{2,1,0:T(8,128)(2,1)} copy(bf16[1,16,3072]{2,1,0:T(8,128)(2,1)} %shard_map.91) | data formatting | bytes 196608
